TPU v7x, 128 devices: a whole 4x4x4 slice. The times are simulated.
128 devices in a mesh: wide: 32 (over y, z, core), narrow: 4 (over x).
Axes of the slice: x: 4, y: 4, z: 4, core: 2. Of those that a mesh axis runs over, the one named last changes fastest.
Arguments:
- frames: bfloat16 [256, 2, 256, 256], P(('wide', 'narrow')), may hold values from -120 to 120
- sketch: bfloat16 [256, 128], replicated, may hold values from -0.3 to 2.3
- kernel_taps: bfloat16 [64], replicated, may hold values from -0.3 to 1.1
Outputs:
- basis: float32 [128, 32768], P(None, ('wide', 'narrow'))
- factor: float32 [128, 128], replicated
All inputs are finite; a program needn't handle non-finite values.
Results may differ from a plain program's by a relative error of at most 0.0043.
Values may be sent and summed in bfloat16 or wider, within the bound.
A program may use at most 64 MiB of HBM per device.

v0:
```python
import jax
import jax.numpy as jnp
from jax import lax
from jax.sharding import PartitionSpec as P


def partner_2(array, axis, bit):
    return lax.ppermute(array, axis, [(i, i ^ 1 << bit) for i in range(lax.axis_size(axis))])


def gauss_taps(spread):
    position = jnp.arange(15, dtype=jnp.float32) - 7.0
    weights = jnp.exp(-position * position / (2.0 * spread * spread))
    return weights / jnp.sum(weights)


def band_matrix(spread, length):
    outputs = length // 2
    offset_index = (
        jnp.arange(length, dtype=jnp.int32)[None, :]
        - 2 * jnp.arange(outputs, dtype=jnp.int32)[:, None]
        + 7
    )
    weights = gauss_taps(spread)
    matrix = jnp.zeros((outputs, length), jnp.float32)
    for offset in range(15):
        matrix = matrix + jnp.where(offset_index == offset, weights[offset], jnp.float32(0.0))
    return matrix


def filter_volumes(frames_block):
    volume = frames_block.astype(jnp.float32)
    row_count = volume.shape[-2]
    col_count = volume.shape[-1]
    half = col_count // 2
    column_bands = jnp.concatenate(
        [band_matrix(1.5, col_count), band_matrix(3.0, col_count)], axis=0
    )
    column_pass = jnp.einsum(
        "...rc,oc->...ro", volume, column_bands, precision=lax.Precision.HIGHEST
    )
    narrow_pass = jnp.einsum(
        "or,...rc->...oc",
        band_matrix(1.5, row_count),
        column_pass[..., :half],
        precision=lax.Precision.HIGHEST,
    )
    broad_pass = jnp.einsum(
        "or,...rc->...oc",
        band_matrix(3.0, row_count),
        column_pass[..., half:],
        precision=lax.Precision.HIGHEST,
    )
    return (narrow_pass - broad_pass).astype(jnp.bfloat16)


def build_toeplitz(kernel_taps, length):
    lag_index = (
        jnp.arange(length, dtype=jnp.int32)[:, None] - jnp.arange(length, dtype=jnp.int32)[None, :]
    )
    toeplitz = jnp.zeros((length, length), jnp.float32)
    for offset in range(kernel_taps.shape[0]):
        toeplitz = toeplitz + jnp.where(
            lag_index == offset, kernel_taps[offset].astype(jnp.float32), jnp.float32(0.0)
        )
    return toeplitz.astype(jnp.bfloat16)


def outer_gram(matrix):
    return lax.dot_general(
        matrix,
        matrix,
        (((1,), (1,)), ((), ())),
        precision=lax.Precision.HIGHEST,
        preferred_element_type=jnp.float32,
    )


def orthonormalize(sketched, voxel_count, group_size):
    gram_part = outer_gram(sketched) / voxel_count
    lower_factor = jnp.linalg.cholesky(gram_part)
    for bit_index in range(group_size.bit_length() - 1):
        partner = partner_2(lower_factor, ("wide", "narrow"), bit_index)
        lower_factor = jnp.linalg.cholesky(outer_gram(lower_factor) + outer_gram(partner))
    basis_rows = jax.scipy.linalg.solve_triangular(lower_factor, sketched, lower=True)
    return (basis_rows, lower_factor.T)


def shards(frames, sketch, kernel_taps):
    filtered = filter_volumes(frames)
    per_device = frames.shape[0]
    flattened = filtered.reshape(per_device, -1)
    voxel_count = flattened.shape[1]
    group_size = lax.axis_size(("wide", "narrow"))
    block = voxel_count // group_size
    length = per_device * group_size
    toeplitz = build_toeplitz(kernel_taps, length)
    arranged = flattened.reshape(1, per_device, group_size, block)
    received = lax.all_to_all(arranged, ("wide", "narrow"), split_axis=2, concat_axis=0, tiled=True)
    deconvolved = jnp.dot(
        toeplitz, received.reshape(length, received.shape[3]), preferred_element_type=jnp.float32
    ).astype(jnp.bfloat16)
    sketched = lax.dot_general(
        sketch, deconvolved, (((0,), (0,)), ((), ())), preferred_element_type=jnp.float32
    )
    deconvolved, sketched = (deconvolved, sketched)
    series = deconvolved.astype(jnp.float32)
    first_basis, unused = orthonormalize(sketched, voxel_count, group_size)
    projected = (
        lax.dot_general(
            series,
            first_basis,
            (((1,), (1,)), ((), ())),
            precision=lax.Precision.HIGHEST,
            preferred_element_type=jnp.float32,
        )
        / voxel_count
    )
    projected = lax.psum(projected, ("wide", "narrow"))
    refined = lax.dot_general(
        projected,
        series,
        (((0,), (0,)), ((), ())),
        precision=lax.Precision.HIGHEST,
        preferred_element_type=jnp.float32,
    )
    basis, factor = orthonormalize(refined, voxel_count, group_size)
    return (basis, factor)


def solution(mesh):
    return jax.shard_map(
        shards,
        mesh=mesh,
        in_specs=(P(("wide", "narrow"), None, None, None), P(), P()),
        out_specs=(P(None, ("wide", "narrow")), P()),
        check_vma=False,
    )
```

profile of v0, /device:TPU:0, one launch (start us, length us, event | category | flops | bytes accessed | tf_op | source)
XLA Modules:
  0.0 561.7 jit_solution(6446294260194581645)
XLA Ops:
  11.2 9.6 %select_add_fusion.1 = f32[128,256]{1,0:T(8,128)S(1)} fusion(f32[]{:T(128)} %bitcast.78, f32[]{:T(128)} %bitcast.77, f32[]{:T(128)} %bitcast.76, f32[]{:T(128)} %bitcast.75, f32[]{:T(128)} %bitcast.74, f32[]{:T(128)} %bitcast.73, f32[]{:T(128)} %bitcast.72, f32[]{:T(128)} %bitcast.71, f32[]{:T(128)} %bitcast.70, f32[]{:T(128)} %bitcast.69, f32[]{:T(128)} %bitcast.68, ...), kind=kLoop, calls=%fused_computation.99 | loop fusion | flops 1507328 | bytes 131644 | tf_op jit(solution)/shard_map/add | solution.py:27
  20.7 9.7 %select_add_fusion = f32[128,256]{1,0:T(8,128)S(1)} fusion(f32[]{:T(128)} %bitcast.93, f32[]{:T(128)} %bitcast.92, f32[]{:T(128)} %bitcast.91, f32[]{:T(128)} %bitcast.90, f32[]{:T(128)} %bitcast.89, f32[]{:T(128)} %bitcast.88, f32[]{:T(128)} %bitcast.87, f32[]{:T(128)} %bitcast.86, f32[]{:T(128)} %bitcast.85, f32[]{:T(128)} %bitcast.84, f32[]{:T(128)} %bitcast.83, ...), kind=kLoop, calls=%fused_computation.98 | loop fusion | flops 1507328 | bytes 131644 | tf_op jit(solution)/shard_map/add | solution.py:27
  31.0 10.2 %fusion.3 = f32[2,2,128,128]{3,2,1,0:T(8,128)S(1)} fusion(f32[2,2,256,256]{2,3,1,0:T(8,128)S(1)} %convolution_bitcast_fusion, f32[]{:T(128)} %bitcast.78, f32[]{:T(128)} %bitcast.77, f32[]{:T(128)} %bitcast.76, f32[]{:T(128)} %bitcast.75, f32[]{:T(128)} %bitcast.74, f32[]{:T(128)} %bitcast.73, f32[]{:T(128)} %bitcast.72, f32[]{:T(128)} %bitcast.71, ...), kind=kOutput, calls=%fused_computation.23 | convolution fusion | flops 202833920 | bytes 787004 | tf_op jit(solution)/shard_map/or,...rc->...oc/dot_general | solution.py:42
  41.2 10.2 %fusion.1 = bf16[2,2,128,128]{2,3,1,0:T(8,128)(2,1)S(1)} fusion(f32[2,2,128,128]{3,2,1,0:T(8,128)S(1)} %fusion.3, f32[2,2,256,256]{2,3,1,0:T(8,128)S(1)} %convolution_bitcast_fusion, f32[]{:T(128)} %bitcast.93, f32[]{:T(128)} %bitcast.92, f32[]{:T(128)} %bitcast.91, f32[]{:T(128)} %bitcast.90, f32[]{:T(128)} %bitcast.89, f32[]{:T(128)} %bitcast.88, ...), kind=kOutput, calls=%fused_computation.4 | convolution fusion | flops 202964992 | bytes 918076 | tf_op jit(solution)/shard_map/or,...rc->...oc/dot_general | solution.py:48
  52.4 11.1 %all-to-all-start = ((bf16[1,2,128,256]{3,1,0,2:T(2,128)(2,1)}), bf16[1,2,128,256]{3,1,0,2:T(2,128)(2,1)S(1)}, u32[]{:S(2)}, u32[]{:S(2)}) async-start(bf16[1,2,128,256]{3,1,0,2:T(2,128)(2,1)} %copy.102), calls=%async_computation | async-start | bytes 262144 | tf_op jit(solution)/shard_map/all_to_all | solution.py:99
  108.4 11.7 %cholesky.254 = f32[128,128]{1,0:T(8,128)S(1)} custom-call(f32[128,128]{1,0:T(8,128)S(1)} %fusion.238), custom_call_target="Cholesky" | custom-call | tf_op jit(solution)/shard_map/jit(cholesky)/cholesky | solution.py:81
  126.7 11.7 %cholesky.265 = f32[128,128]{1,0:T(8,128)S(1)} custom-call(f32[128,128]{1,0:T(8,128)S(1)} %fusion.237), custom_call_target="Cholesky" | custom-call | tf_op jit(solution)/shard_map/jit(cholesky)/cholesky | solution.py:84
  146.0 11.7 %cholesky.276 = f32[128,128]{1,0:T(8,128)S(1)} custom-call(f32[128,128]{1,0:T(8,128)S(1)} %fusion.236), custom_call_target="Cholesky" | custom-call | tf_op jit(solution)/shard_map/jit(cholesky)/cholesky | solution.py:84
  161.0 11.7 %cholesky.287 = f32[128,128]{1,0:T(8,128)S(1)} custom-call(f32[128,128]{1,0:T(8,128)S(1)} %fusion.235), custom_call_target="Cholesky" | custom-call | tf_op jit(solution)/shard_map/jit(cholesky)/cholesky | solution.py:84
  178.7 11.7 %cholesky.298 = f32[128,128]{1,0:T(8,128)S(1)} custom-call(f32[128,128]{1,0:T(8,128)S(1)} %fusion.234), custom_call_target="Cholesky" | custom-call | tf_op jit(solution)/shard_map/jit(cholesky)/cholesky | solution.py:84
  198.2 11.7 %cholesky.309 = f32[128,128]{1,0:T(8,128)S(1)} custom-call(f32[128,128]{1,0:T(8,128)S(1)} %fusion.233), custom_call_target="Cholesky" | custom-call | tf_op jit(solution)/shard_map/jit(cholesky)/cholesky | solution.py:84
  216.0 11.7 %cholesky.320 = f32[128,128]{1,0:T(8,128)S(1)} custom-call(f32[128,128]{1,0:T(8,128)S(1)} %fusion.232), custom_call_target="Cholesky" | custom-call | tf_op jit(solution)/shard_map/jit(cholesky)/cholesky | solution.py:84
  235.7 11.7 %cholesky.331 = f32[128,128]{1,0:T(8,128)S(1)} custom-call(f32[128,128]{1,0:T(8,128)S(1)} %fusion.231), custom_call_target="Cholesky" | custom-call | tf_op jit(solution)/shard_map/jit(cholesky)/cholesky | solution.py:84
  248.8 9.8 %custom-call.6 = f32[1,128,128]{1,2,0:T(8,128)S(1)} custom-call(f32[1,128,128]{2,1,0:T(8,128)S(1)} %fusion.219), custom_call_target="InvertDiagBlocksLowerTriangular" | custom-call | tf_op jit(solution)/shard_map/jit(_solve_triangular)/triangular_solve | solution.py:85
  259.9 141.4 %all-reduce.2.cloned.1.call-done = f32[256,128]{1,0:T(8,128)} async-done(((f32[256,128]{1,0:T(8,128)}), f32[256,128]{1,0:T(8,128)}) %all-reduce.2.cloned.1.call-update) | async-done | bytes 131088 | tf_op jit(solution)/shard_map/psum | solution.py:119
  402.9 11.7 %cholesky.342 = f32[128,128]{1,0:T(8,128)S(1)} custom-call(f32[128,128]{1,0:T(8,128)S(1)} %fusion.229), custom_call_target="Cholesky" | custom-call | tf_op jit(solution)/shard_map/jit(cholesky)/cholesky | solution.py:81
  420.8 11.7 %cholesky.353 = f32[128,128]{1,0:T(8,128)S(1)} custom-call(f32[128,128]{1,0:T(8,128)S(1)} %fusion.228), custom_call_target="Cholesky" | custom-call | tf_op jit(solution)/shard_map/jit(cholesky)/cholesky | solution.py:84
  440.1 11.7 %cholesky.364 = f32[128,128]{1,0:T(8,128)S(1)} custom-call(f32[128,128]{1,0:T(8,128)S(1)} %fusion.227), custom_call_target="Cholesky" | custom-call | tf_op jit(solution)/shard_map/jit(cholesky)/cholesky | solution.py:84
  455.1 11.7 %cholesky.375 = f32[128,128]{1,0:T(8,128)S(1)} custom-call(f32[128,128]{1,0:T(8,128)S(1)} %fusion.226), custom_call_target="Cholesky" | custom-call | tf_op jit(solution)/shard_map/jit(cholesky)/cholesky | solution.py:84
  472.9 11.7 %cholesky.386 = f32[128,128]{1,0:T(8,128)S(1)} custom-call(f32[128,128]{1,0:T(8,128)S(1)} %fusion.225), custom_call_target="Cholesky" | custom-call | tf_op jit(solution)/shard_map/jit(cholesky)/cholesky | solution.py:84
  492.4 11.7 %cholesky.397 = f32[128,128]{1,0:T(8,128)S(1)} custom-call(f32[128,128]{1,0:T(8,128)S(1)} %fusion.224), custom_call_target="Cholesky" | custom-call | tf_op jit(solution)/shard_map/jit(cholesky)/cholesky | solution.py:84
  510.2 11.7 %cholesky.408 = f32[128,128]{1,0:T(8,128)S(1)} custom-call(f32[128,128]{1,0:T(8,128)S(1)} %fusion.223), custom_call_target="Cholesky" | custom-call | tf_op jit(solution)/shard_map/jit(cholesky)/cholesky | solution.py:84
  529.8 11.7 %cholesky.419 = f32[128,128]{1,0:T(8,128)S(1)} custom-call(f32[128,128]{1,0:T(8,128)S(1)} %fusion.222), custom_call_target="Cholesky" | custom-call | tf_op jit(solution)/shard_map/jit(cholesky)/cholesky | solution.py:84
  542.9 9.8 %custom-call.7 = f32[1,128,128]{1,2,0:T(8,128)S(1)} custom-call(f32[1,128,128]{2,1,0:T(8,128)S(1)} %get-tuple-element.11), custom_call_target="InvertDiagBlocksLowerTriangular" | custom-call | tf_op jit(solution)/shard_map/jit(_solve_triangular)/triangular_solve | solution.py:85
  (170 shorter events, 107.3 us)
Async XLA Ops:
  7.2 23.2 %copy-start = (bf16[2,2,256,256]{3,2,1,0:T(8,128)(2,1)S(1)}, bf16[2,2,256,256]{3,2,1,0:T(8,128)(2,1)}, u32[]{:S(2)}) copy-start(bf16[2,2,256,256]{3,2,1,0:T(8,128)(2,1)} %param.6) | copy-start | bytes 1572868
  52.4 11.2 %copy-start.1 = (bf16[64]{0:T(256)(128)(2,1)S(1)}, bf16[64]{0:T(256)(128)(2,1)}, u32[]{:S(2)}) copy-start(bf16[64]{0:T(256)(128)(2,1)} %param.8) | copy-start | bytes 388
  52.4 54.2 %all-to-all-start = ((bf16[1,2,128,256]{3,1,0,2:T(2,128)(2,1)}), bf16[1,2,128,256]{3,1,0,2:T(2,128)(2,1)S(1)}, u32[]{:S(2)}, u32[]{:S(2)}) async-start(bf16[1,2,128,256]{3,1,0,2:T(2,128)(2,1)} %copy.102), calls=%async_computation | async-start | bytes 262144 | tf_op jit(solution)/shard_map/all_to_all | solution.py:99
  63.6 337.7 %all-reduce.2.cloned.1.call-start = ((), (), s32[]{:S(2)}) async-start(), calls=%async_computation.1 | async-start | bytes 262144 | tf_op jit(solution)/shard_map/psum | solution.py:119
  106.7 1.0 copy-start.2
  121.5 4.9 collective-permute-start
  139.8 5.8 %collective-permute-start.1 = (f32[128,128]{1,0:T(8,128)S(1)}, f32[128,128]{1,0:T(8,128)S(1)}, u32[]{:S(2)}, u32[]{:S(2)}) collective-permute-start(f32[128,128]{1,0:T(8,128)S(1)} %fusion.239), channel_id=1, source_target_pairs={{0,2},{1,3},{2,0},{3,1},{4,6},{5,7},{6,4},{7,5},{8,10},{9,11},{10,... | collective-permute-start | bytes 196616 | tf_op jit(solution)/shard_map/ppermute | solution.py:8
  159.1 1.5 collective-permute-start.2
  174.0 4.3 collective-permute-start.3
  191.8 6.1 %collective-permute-start.4 = (f32[128,128]{1,0:T(8,128)S(1)}, f32[128,128]{1,0:T(8,128)S(1)}, u32[]{:S(2)}, u32[]{:S(2)}) collective-permute-start(f32[128,128]{1,0:T(8,128)S(1)} %fusion.242), channel_id=1, source_target_pairs={{0,16},{1,17},{2,18},{3,19},{4,20},{5,21},{6,22},{7,23},{8,24},{9,... | collective-permute-start | bytes 196616 | tf_op jit(solution)/shard_map/ppermute | solution.py:8
  211.3 4.3 collective-permute-start.5
  229.1 6.3 %collective-permute-start.6 = (f32[128,128]{1,0:T(8,128)S(1)}, f32[128,128]{1,0:T(8,128)S(1)}, u32[]{:S(2)}, u32[]{:S(2)}) collective-permute-start(f32[128,128]{1,0:T(8,128)S(1)} %fusion.244), channel_id=1, source_target_pairs={{0,64},{1,65},{2,66},{3,67},{4,68},{5,69},{6,70},{7,71},{8,72},{9,... | collective-permute-start | bytes 196616 | tf_op jit(solution)/shard_map/ppermute | solution.py:8
  415.9 4.5 collective-permute-start.7
  433.9 5.8 %collective-permute-start.8 = (f32[128,128]{1,0:T(8,128)S(1)}, f32[128,128]{1,0:T(8,128)S(1)}, u32[]{:S(2)}, u32[]{:S(2)}) collective-permute-start(f32[128,128]{1,0:T(8,128)S(1)} %fusion.247), channel_id=1, source_target_pairs={{0,2},{1,3},{2,0},{3,1},{4,6},{5,7},{6,4},{7,5},{8,10},{9,11},{10,... | collective-permute-start | bytes 196616 | tf_op jit(solution)/shard_map/ppermute | solution.py:8
  453.2 1.5 collective-permute-start.9
  468.2 4.3 collective-permute-start.10
  486.0 6.1 %collective-permute-start.11 = (f32[128,128]{1,0:T(8,128)S(1)}, f32[128,128]{1,0:T(8,128)S(1)}, u32[]{:S(2)}, u32[]{:S(2)}) collective-permute-start(f32[128,128]{1,0:T(8,128)S(1)} %fusion.250), channel_id=1, source_target_pairs={{0,16},{1,17},{2,18},{3,19},{4,20},{5,21},{6,22},{7,23},{8,24},{9,... | collective-permute-start | bytes 196616 | tf_op jit(solution)/shard_map/ppermute | solution.py:8
  505.5 4.3 collective-permute-start.12
  523.3 6.1 %collective-permute-start.13 = (f32[128,128]{1,0:T(8,128)S(1)}, f32[128,128]{1,0:T(8,128)S(1)}, u32[]{:S(2)}, u32[]{:S(2)}) collective-permute-start(f32[128,128]{1,0:T(8,128)S(1)} %fusion.252), channel_id=1, source_target_pairs={{0,64},{1,65},{2,66},{3,67},{4,68},{5,69},{6,70},{7,71},{8,72},{9,... | collective-permute-start | bytes 196616 | tf_op jit(solution)/shard_map/ppermute | solution.py:8
Sparse Core Ops, SparseCore 0:
  260.0 141.2 all-reduce.1
where the time goes:
time: 570 us; the launch traced here: 562 us
  other arithmetic  250 us (44%)
  waiting for transfers between devices  181 us (32%)
  between operations  55.2 us (10%)
  starting transfers between devices  34.1 us (6%)
  matrix products  33.7 us (6%)
  local copies, waits for them, and re-layouts  7.52 us (1%)
    another operation x42, other arithmetic, orthonormalize(): jnp.linalg.cholesky(outer_gram(lower_factor) + outer_gram(partner))  173 us
    psum x1, waiting for transfers between devices, shards(): projected = lax.psum(projected, ('wide', 'narrow'))  141 us
    ppermute x14, waiting for transfers between devices, partner_2(): lax.ppermute(array, axis, [(i, i ^ 1 << bit) for i in range(lax.axis_size...  39.5 us
    another operation x6, other arithmetic, orthonormalize(): lower_factor = jnp.linalg.cholesky(gram_part)  24.8 us
    ppermute x14, starting transfers between devices, partner_2(): lax.ppermute(array, axis, [(i, i ^ 1 << bit) for i in range(lax.axis_size...  22.9 us
    another operation x3, other arithmetic, orthonormalize(): jax.scipy.linalg.solve_triangular(lower_factor, sketched, lower=True)  20.3 us
    add x2, other arithmetic, band_matrix(): matrix + jnp.where(offset_index == offset, weights[offset], jnp.float32(0...  19.2 us
  transfers between devices with their start and end apart: 16, of which 15 were waited for; matrix products, arithmetic and copies ran while one was open for 1% of the time, Pallas kernels for 0%

commit v1 on v0

v1 whole, which is shorter than its diff:
```python
import functools

import jax
import jax.numpy as jnp
import numpy as np
from jax import lax
from jax.experimental import pallas as pl
from jax.experimental.pallas import tpu as pltpu
from jax.sharding import PartitionSpec as P

MESH = pl.DeviceIdType.MESH
F32 = jnp.float32
BF16 = jnp.bfloat16


def gauss_band(spread, length):
    position = np.arange(15, dtype=np.float64) - 7.0
    weights = np.exp(-position * position / (2.0 * spread * spread))
    weights = weights / weights.sum()
    matrix = np.zeros((length // 2, length), np.float64)
    for o in range(length // 2):
        for k in range(15):
            c = 2 * o + k - 7
            if 0 <= c < length:
                matrix[o, c] = weights[k]
    return matrix


def split2(matrix):
    hi = matrix.astype(BF16)
    lo = (matrix - hi.astype(F32)).astype(BF16)
    return hi, lo


def split3(matrix):
    hi = matrix.astype(BF16)
    rest = matrix - hi.astype(F32)
    mid = rest.astype(BF16)
    lo = (rest - mid.astype(F32)).astype(BF16)
    return hi, mid, lo


def np_split2(matrix):
    hi = matrix.astype(BF16)
    lo = (matrix - hi.astype(np.float64)).astype(BF16)
    return hi, lo


def dot(a, b, ca=1, cb=0):
    return lax.dot_general(a, b, (((ca,), (cb,)), ((), ())), preferred_element_type=F32)


def dot_ff(a, b, ca=1, cb=0):
    ah, al = split2(a)
    bh, bl = split2(b)
    return dot(ah, bh, ca, cb) + (dot(ah, bl, ca, cb) + dot(al, bh, ca, cb))


def dot_fb(a, b, ca=1, cb=0):
    hi, mid, lo = split3(a)
    return dot(hi, b, ca, cb) + (dot(mid, b, ca, cb) + dot(lo, b, ca, cb))


def exchange_kernel(
    n_wide, n_narrow, frames_ref, taps_ref, colh_ref, coll_ref, rowh_ref, rowl_ref,
    gram_ref, series_ref,
    tap_row, tx, rx, gtx, grx, gall, send_sems, recv_sems,
):
    n = n_wide * n_narrow
    me = lax.axis_index("wide") * n_narrow + lax.axis_index("narrow")

    def peer(i):
        p = lax.rem(me + i, n)
        return p, (p // n_narrow, lax.rem(p, n_narrow))

    barrier = pltpu.get_barrier_semaphore()

    def greet(i, carry):
        _, device = peer(i)
        pl.semaphore_signal(barrier, inc=1, device_id=device, device_id_type=MESH)
        return carry

    lax.fori_loop(1, n, greet, 0)

    x = frames_ref[...].reshape(2 * 2 * 256, 256)
    y = dot(x, colh_ref[...]) + dot(x, coll_ref[...])
    for p in range(2):
        a = y[p * 256 : (p + 1) * 256]
        b = y[(p + 2) * 256 : (p + 3) * 256]
        right = jnp.concatenate(
            [
                jnp.concatenate([a[:, :128], b[:, :128]], axis=1),
                jnp.concatenate([a[:, 128:], b[:, 128:]], axis=1),
            ],
            axis=0,
        )
        rh, rl = split2(right)
        out = dot(rowh_ref[...], rh) + (dot(rowh_ref[...], rl) + dot(rowl_ref[...], rh))
        out = out.astype(BF16).astype(F32)
        for h in range(2):
            tx[p * 64 : (p + 1) * 64, 0, h * 256 : (h + 1) * 256] = out[h * 64 : (h + 1) * 64]

    pl.semaphore_wait(barrier, n - 1)

    def push(src, dst, slot):
        def body(i, carry):
            p, device = peer(i)
            pltpu.make_async_remote_copy(
                src_ref=src.at[p],
                dst_ref=dst.at[me],
                send_sem=send_sems.at[slot],
                recv_sem=recv_sems.at[slot],
                device_id=device,
                device_id_type=MESH,
            ).start()
            return carry

        lax.fori_loop(1, n, body, 0)

    def wait(ref, sem):
        part = ref.at[pl.ds(0, n - 1)]
        pltpu.make_async_copy(part, part, sem).wait()

    push(tx, rx, 0)
    rx[me] = tx[me]

    tap_row[...] = jnp.zeros_like(tap_row)
    tap_row[0:1, 0:64] = taps_ref[...].astype(F32)
    base = jnp.broadcast_to(tap_row[0:1, :], (128, 256))
    s_index = lax.broadcasted_iota(jnp.int32, (128, 256), 0)
    t_index = lax.broadcasted_iota(jnp.int32, (128, 256), 1)
    halves = []
    for v in range(2):
        rolled = pltpu.roll(base, v, 1, stride=2, stride_axis=0)
        halves.append(jnp.where(t_index >= 2 * s_index + v, rolled, 0.0))
    toeplitz = jnp.concatenate(halves, axis=0).astype(BF16)

    wait(rx, recv_sems.at[0])
    columns = [
        jnp.concatenate([rx[:, 0, (2 * h + v) * 128 : (2 * h + v + 1) * 128] for v in range(2)], axis=0)
        for h in range(2)
    ]
    received = jnp.concatenate(columns, axis=1).astype(BF16)
    series = dot(toeplitz, received, 0, 0).astype(BF16)
    series_ref[...] = series
    part = dot(series, series, 1, 1)
    gtx[:, 0, 0:128] = part[0:128, 0:128]
    gtx[:, 0, 128:256] = part[128:256, 0:128]
    gtx[:, 0, 256:384] = part[128:256, 128:256]
    push(gtx, grx, 1)
    grx[me] = gtx[me]
    wait(grx, recv_sems.at[1])
    gall[me] = jnp.sum(grx[...], axis=0)

    def share(i, carry):
        _, device = peer(i)
        pltpu.make_async_remote_copy(
            src_ref=gall.at[me],
            dst_ref=gall.at[me],
            send_sem=send_sems.at[2],
            recv_sem=recv_sems.at[2],
            device_id=device,
            device_id_type=MESH,
        ).start()
        return carry

    lax.fori_loop(1, n, share, 0)
    wait(gall, recv_sems.at[2])
    gram_ref[...] = gall[:, 0, :] * (1.0 / 32768.0)
    wait(tx, send_sems.at[0])
    wait(gtx, send_sems.at[1])
    wait(gall, send_sems.at[2])


def eliminate(matrices):
    size = matrices[0].shape[0]
    r = lax.broadcasted_iota(jnp.int32, (size, size), 0)
    c = lax.broadcasted_iota(jnp.int32, (size, size), 1)
    eye = jnp.where(r == c, 1.0, 0.0).astype(F32)
    sub = lax.broadcasted_iota(jnp.int32, (8, 1), 0)
    work = []
    for g in matrices:
        m = jnp.concatenate([g, eye], axis=1)
        work.append([m[8 * i : 8 * i + 8] for i in range(size // 8)])
    for k in range(size):
        t, s = divmod(k, 8)
        for rows in work:
            row = rows[t][s : s + 1, :]
            scaled = row * (1.0 / row[:, k : k + 1])
            for i in range(t, size // 8):
                f = rows[i][:, k : k + 1]
                if i == t:
                    f = jnp.where(sub > s, f, 0.0)
                rows[i] = rows[i] - f * scaled
    results = []
    for rows in work:
        m = jnp.concatenate(rows, axis=0)
        upper = jnp.where(c >= r, m[:, :size], 0.0)
        diagonal = jnp.sum(jnp.where(r == c, upper, 0.0), axis=1, keepdims=True)
        scale = lax.rsqrt(diagonal)
        results.append((upper * scale, m[:, size:] * scale))
    return results


def factor_kernel(gram_ref, series_ref, sketch_ref, basis_ref, factor_ref):
    c11 = gram_ref[:, 0:128]
    c21 = gram_ref[:, 128:256]
    c22 = gram_ref[:, 256:384]
    cov = jnp.concatenate(
        [jnp.concatenate([c11, c21.T], axis=1), jnp.concatenate([c21, c22], axis=1)], axis=0
    )
    sketch = sketch_ref[...]
    w = dot_fb(cov, sketch)
    g1 = dot_fb(w, sketch, 0, 0).T
    cw = dot_ff(cov, w)
    g2 = dot_ff(w, cw, 0, 0)
    (_, inv1), (up2, inv2) = eliminate([g1, g2])
    factor_ref[...] = dot_ff(up2, inv1, 1, 1)
    z = dot_ff(inv2, w, 1, 1)
    basis_ref[...] = dot_fb(z, series_ref[...])


def shards(n_wide, n_narrow, frames, sketch, kernel_taps):
    n = n_wide * n_narrow
    narrow_band, broad_band = gauss_band(1.5, 256), gauss_band(3.0, 256)
    colh, coll = np_split2(np.concatenate([narrow_band, broad_band], axis=0).T)
    order = np.concatenate([np.arange(0, 128, 2), np.arange(1, 128, 2)])
    rowh, rowl = np_split2(np.concatenate([narrow_band, -broad_band], axis=1)[order])
    vmem = pl.BlockSpec(memory_space=pltpu.VMEM)
    gram, series = pl.pallas_call(
        functools.partial(exchange_kernel, n_wide, n_narrow),
        out_shape=(
            jax.ShapeDtypeStruct((128, 384), F32),
            jax.ShapeDtypeStruct((256, 256), BF16),
        ),
        in_specs=[vmem] * 6,
        out_specs=(vmem, vmem),
        scratch_shapes=[
            pltpu.VMEM((8, 256), F32),
            pltpu.VMEM((n, 1, 512), F32),
            pltpu.VMEM((n, 1, 512), F32),
            pltpu.VMEM((n, 1, 384), F32),
            pltpu.VMEM((n, 1, 384), F32),
            pltpu.VMEM((n, 1, 384), F32),
            pltpu.SemaphoreType.DMA((3,)),
            pltpu.SemaphoreType.DMA((3,)),
        ],
        compiler_params=pltpu.CompilerParams(
            collective_id=0, has_side_effects=True, vmem_limit_bytes=40 * 2**20
        ),
        name="exchange",
    )(
        frames, kernel_taps.reshape(1, 64),
        jnp.asarray(colh), jnp.asarray(coll), jnp.asarray(rowh), jnp.asarray(rowl),
    )
    return pl.pallas_call(
        factor_kernel,
        out_shape=(jax.ShapeDtypeStruct((128, 256), F32), jax.ShapeDtypeStruct((128, 128), F32)),
        in_specs=[vmem] * 3,
        out_specs=(vmem, vmem),
        compiler_params=pltpu.CompilerParams(vmem_limit_bytes=40 * 2**20),
        name="factorize",
    )(gram, series, sketch)


def solution(mesh):
    return jax.shard_map(
        functools.partial(shards, mesh.shape["wide"], mesh.shape["narrow"]),
        mesh=mesh,
        in_specs=(P(("wide", "narrow"), None, None, None), P(), P()),
        out_specs=(P(None, ("wide", "narrow")), P()),
        check_vma=False,
    )
```

time: 570 us -> 52 us (0.09)
  the two profiles are of different devices: /device:TPU:0 before, /device:TPU:1 now
where the time goes in v1:
time: 52 us; the launch traced here: 51.7 us
  Pallas kernels  45.8 us (88%)
  local copies, waits for them, and re-layouts  5.31 us (10%)
  between operations  0.66 us (1%)
    pallas_call x1, Pallas kernels, shards(): pl.pallas_call(functools.partial(exchange_kernel, n_wide, n_narrow), out_...  32.8 us
    pallas_call x1, Pallas kernels, shards(): pl.pallas_call(factor_kernel, out_shape=(jax.ShapeDtypeStruct((128, 256),...  12.9 us
    unnamed x14, local copies, waits for them, and re-layouts  5.31 us

profile of v1, /device:TPU:1, one launch (start us, length us, event | category | flops | bytes accessed | tf_op | source)
XLA Modules:
  0.0 51.7 jit_solution(133488694106104283)
XLA Ops:
  0.6 0.0 copy-start.6
  0.6 0.6 %copy-done.6 = bf16[64]{0:T(256)(128)(2,1)S(1)} copy-done((bf16[64]{0:T(256)(128)(2,1)S(1)}, bf16[64]{0:T(256)(128)(2,1)}, u32[]{:S(2)}) %copy-start.6) | copy-done | bytes 152
  1.3 0.0 copy-start
  1.3 1.0 %copy-done = bf16[2,2,256,256]{3,2,1,0:T(8,128)(2,1)S(1)} copy-done((bf16[2,2,256,256]{3,2,1,0:T(8,128)(2,1)S(1)}, bf16[2,2,256,256]{3,2,1,0:T(8,128)(2,1)}, u32[]{:S(2)}) %copy-start) | copy-done | bytes 524312
  2.3 0.0 copy-start.1
  2.3 0.9 %copy-done.1 = bf16[128,512]{1,0:T(8,128)(2,1)S(1)} copy-done((bf16[128,512]{1,0:T(8,128)(2,1)S(1)}, bf16[128,512]{1,0:T(8,128)(2,1)}, u32[]{:S(2)}) %copy-start.1) | copy-done | bytes 131096
  3.2 0.0 copy-start.2
  3.2 0.9 %copy-done.2 = bf16[128,512]{1,0:T(8,128)(2,1)S(1)} copy-done((bf16[128,512]{1,0:T(8,128)(2,1)S(1)}, bf16[128,512]{1,0:T(8,128)(2,1)}, u32[]{:S(2)}) %copy-start.2) | copy-done | bytes 131096
  4.1 0.0 copy-start.3
  4.1 0.9 %copy-done.3 = bf16[256,256]{1,0:T(8,128)(2,1)S(1)} copy-done((bf16[256,256]{1,0:T(8,128)(2,1)S(1)}, bf16[256,256]{1,0:T(8,128)(2,1)}, u32[]{:S(2)}) %copy-start.3) | copy-done | bytes 131096
  5.0 0.0 copy-start.4
  5.0 0.9 %copy-done.4 = bf16[256,256]{1,0:T(8,128)(2,1)S(1)} copy-done((bf16[256,256]{1,0:T(8,128)(2,1)S(1)}, bf16[256,256]{1,0:T(8,128)(2,1)}, u32[]{:S(2)}) %copy-start.4) | copy-done | bytes 131096
  5.9 0.0 copy-start.5
  5.9 32.8 %exchange.1 = (f32[128,384]{1,0:T(8,128)S(1)}, bf16[256,256]{1,0:T(8,128)(2,1)S(1)}) custom-call(bf16[2,2,256,256]{3,2,1,0:T(8,128)(2,1)S(1)} %copy-done, bf16[1,64]{1,0:T(2,128)(2,1)S(1)} %bitcast.1, bf16[256,256]{1,0:T(8,128)(2,1)S(1)} %copy-done.4, bf16[256,256]{1,0:T(8,128)(2,1)S(1)} %copy-done.3, bf16[128,512]{1,0:T(8,128)(2,1)S(1)} %copy-done.2, ...), custom_call_target="tpu_custom_call" | custom-call | tf_op jit(solution)/shard_map/exchange/pallas_call | solution.py:230
  38.8 0.0 copy-done.5
  38.8 12.9 %factorize.1 = (f32[128,256]{1,0:T(8,128)}, f32[128,128]{1,0:T(8,128)}) custom-call(f32[128,384]{1,0:T(8,128)S(1)} %get-tuple-element.4.gram_ref, bf16[256,256]{1,0:T(8,128)(2,1)S(1)} %get-tuple-element.5.series_ref, bf16[256,128]{1,0:T(8,128)(2,1)S(1)} %copy-done.5), custom_call_target="tpu_custom_call" | custom-call | tf_op jit(solution)/shard_map/factorize/pallas_call | solution.py:256
Async XLA Ops:
  0.6 0.7 %copy-start.6 = (bf16[64]{0:T(256)(128)(2,1)S(1)}, bf16[64]{0:T(256)(128)(2,1)}, u32[]{:S(2)}) copy-start(bf16[64]{0:T(256)(128)(2,1)} %param.9) | copy-start | bytes 388
  1.3 1.0 %copy-start = (bf16[2,2,256,256]{3,2,1,0:T(8,128)(2,1)S(1)}, bf16[2,2,256,256]{3,2,1,0:T(8,128)(2,1)}, u32[]{:S(2)}) copy-start(bf16[2,2,256,256]{3,2,1,0:T(8,128)(2,1)} %frames_ref.1) | copy-start | bytes 1572868
  2.3 0.9 %copy-start.1 = (bf16[128,512]{1,0:T(8,128)(2,1)S(1)}, bf16[128,512]{1,0:T(8,128)(2,1)}, u32[]{:S(2)}) copy-start(bf16[128,512]{1,0:T(8,128)(2,1)} %constant.11.clone.rowl_ref) | copy-start | bytes 393220
  3.2 0.9 %copy-start.2 = (bf16[128,512]{1,0:T(8,128)(2,1)S(1)}, bf16[128,512]{1,0:T(8,128)(2,1)}, u32[]{:S(2)}) copy-start(bf16[128,512]{1,0:T(8,128)(2,1)} %constant.10.clone.rowh_ref) | copy-start | bytes 393220
  4.1 0.9 %copy-start.3 = (bf16[256,256]{1,0:T(8,128)(2,1)S(1)}, bf16[256,256]{1,0:T(8,128)(2,1)}, u32[]{:S(2)}) copy-start(bf16[256,256]{1,0:T(8,128)(2,1)} %constant.9.clone.coll_ref) | copy-start | bytes 393220
  5.0 0.9 %copy-start.4 = (bf16[256,256]{1,0:T(8,128)(2,1)S(1)}, bf16[256,256]{1,0:T(8,128)(2,1)}, u32[]{:S(2)}) copy-start(bf16[256,256]{1,0:T(8,128)(2,1)} %constant.8.clone.colh_ref) | copy-start | bytes 393220
  5.9 32.8 %copy-start.5 = (bf16[256,128]{1,0:T(8,128)(2,1)S(1)}, bf16[256,128]{1,0:T(8,128)(2,1)}, u32[]{:S(2)}) copy-start(bf16[256,128]{1,0:T(8,128)(2,1)} %sketch_ref.1) | copy-start | bytes 196612

commit v2 on v1

v2 whole, which is shorter than its diff:
```python
import jax
import jax.numpy as jnp
import numpy as np
from jax import lax
from jax.experimental import pallas as pl
from jax.experimental.pallas import tpu as pltpu
from jax.sharding import PartitionSpec as P

MESH = pl.DeviceIdType.MESH
F32 = jnp.float32
BF16 = jnp.bfloat16


def gauss_band(spread, length):
    position = np.arange(15, dtype=np.float64) - 7.0
    weights = np.exp(-position * position / (2.0 * spread * spread))
    weights = weights / weights.sum()
    matrix = np.zeros((length // 2, length), np.float64)
    for o in range(length // 2):
        for k in range(15):
            c = 2 * o + k - 7
            if 0 <= c < length:
                matrix[o, c] = weights[k]
    return matrix


def split2(matrix):
    hi = matrix.astype(BF16)
    lo = (matrix - hi.astype(F32)).astype(BF16)
    return hi, lo


def split3(matrix):
    hi = matrix.astype(BF16)
    rest = matrix - hi.astype(F32)
    mid = rest.astype(BF16)
    lo = (rest - mid.astype(F32)).astype(BF16)
    return hi, mid, lo


def np_split2(matrix):
    hi = matrix.astype(BF16)
    lo = (matrix - hi.astype(np.float64)).astype(BF16)
    return hi, lo


def dot(a, b, ca=1, cb=0):
    return lax.dot_general(a, b, (((ca,), (cb,)), ((), ())), preferred_element_type=F32)


def dot_ff(a, b, ca=1, cb=0):
    ah, am, al = split3(a)
    bh, bm, bl = split3(b)
    first = dot(ah, bm, ca, cb) + dot(am, bh, ca, cb)
    second = dot(ah, bl, ca, cb) + dot(am, bm, ca, cb) + dot(al, bh, ca, cb)
    return dot(ah, bh, ca, cb) + (first + second)


def dot_fb(a, b, ca=1, cb=0):
    hi, mid, lo = split3(a)
    return dot(hi, b, ca, cb) + (dot(mid, b, ca, cb) + dot(lo, b, ca, cb))


def hops(*offsets):
    return sum(min(o % 4, -o % 4) for o in offsets)


YZ = sorted(((y, z) for y in range(4) for z in range(4) if y or z), key=lambda s: -hops(*s))
CX = sorted(((c, x) for c in range(2) for x in range(4) if c or x), key=lambda s: (-hops(s[1]), -s[0]))


def exchange_kernel(
    frames_hbm, taps_hbm, bands_hbm,
    gram_ref, series_ref,
    frames_ref, taps_ref, bands_ref, load_sems, tap_row,
    tx, rx, tx2, rx2, gtx, grx, atx, arx, gall, send_sems, recv_sems,
):
    wide, x_me = lax.axis_index("wide"), lax.axis_index("narrow")
    y_me, z_me, c_me = wide // 8, lax.rem(wide // 2, 4), lax.rem(wide, 2)
    yz_me, cx_me = wide // 2, c_me * 4 + x_me

    def yz_peers():
        for dy, dz in YZ:
            yz = lax.rem(y_me + dy, 4) * 4 + lax.rem(z_me + dz, 4)
            yield yz, (yz * 2 + c_me, x_me)

    def cx_peers():
        for dc, dx in CX:
            c, x = lax.rem(c_me + dc, 2), lax.rem(x_me + dx, 4)
            yield c * 4 + x, (yz_me * 2 + c, x)

    loads = [
        pltpu.make_async_copy(src, dst, load_sems.at[i])
        for i, (src, dst) in enumerate(
            [(frames_hbm, frames_ref), (bands_hbm, bands_ref), (taps_hbm, taps_ref)]
        )
    ]
    for load in loads:
        load.start()

    barrier = pltpu.get_barrier_semaphore()
    for peers in (yz_peers, cx_peers):
        for _, device in peers():
            pl.semaphore_signal(barrier, inc=1, device_id=device, device_id_type=MESH)

    def push(peers, src, dst, slot):
        for p, device in peers():
            pltpu.make_async_remote_copy(
                src_ref=src(p),
                dst_ref=dst,
                send_sem=send_sems.at[slot],
                recv_sem=recv_sems.at[slot],
                device_id=device,
                device_id_type=MESH,
            ).start()

    def wait(ref, count, sem):
        part = ref.at[pl.ds(0, count)]
        pltpu.make_async_copy(part, part, sem).wait()

    for load in loads:
        load.wait()
    colh, coll = bands_ref[0:256, 0:256], bands_ref[0:256, 256:512]
    rowh, rowl = bands_ref[256:384, :], bands_ref[384:512, :]
    x = frames_ref[...].reshape(2 * 2 * 256, 256)
    y = dot(x, colh) + dot(x, coll)
    for p in range(2):
        a = y[p * 256 : (p + 1) * 256]
        b = y[(p + 2) * 256 : (p + 3) * 256]
        right = jnp.concatenate(
            [
                jnp.concatenate([a[:, :128], b[:, :128]], axis=1),
                jnp.concatenate([a[:, 128:], b[:, 128:]], axis=1),
            ],
            axis=0,
        )
        rh, rl = split2(right)
        out = dot(rowh, rh) + (dot(rowh, rl) + dot(rowl, rh))
        tx[8 * p : 8 * p + 8] = out.astype(BF16).reshape(8, 16, 256)

    pl.semaphore_wait(barrier, len(YZ) + len(CX))
    push(yz_peers, lambda p: tx.at[p], rx.at[yz_me], 0)
    rx[yz_me] = tx[yz_me]

    r = lax.broadcasted_iota(jnp.int32, (256, 256), 0)
    c = lax.broadcasted_iota(jnp.int32, (256, 256), 1)
    reorder = jnp.where(c == (r % 16) * 16 + r // 16, 1.0, 0.0).astype(BF16)

    tap_row[...] = jnp.zeros_like(tap_row)
    tap_row[0:1, 0:64] = taps_ref[...].astype(F32)
    base = jnp.broadcast_to(tap_row[0:1, :], (16, 256))
    s_index = lax.broadcasted_iota(jnp.int32, (16, 256), 0)
    t_index = lax.broadcasted_iota(jnp.int32, (16, 256), 1)
    pieces = []
    for v in range(2):
        for cx in range(8):
            rolled = pltpu.roll(base, 2 * cx + v, 1, stride=16, stride_axis=0)
            pieces.append(jnp.where(t_index >= 16 * s_index + 2 * cx + v, rolled, 0.0))
    toeplitz = jnp.concatenate(pieces, axis=0).astype(BF16)

    wait(rx, len(YZ), recv_sems.at[0])
    tx2[...] = dot(reorder, rx[...].reshape(256, 256)).astype(BF16).reshape(8, 32, 256)
    push(cx_peers, lambda p: tx2.at[p], rx2.at[cx_me], 1)
    rx2[cx_me] = tx2[cx_me]
    wait(rx2, len(CX), recv_sems.at[1])
    halves = [rx2[:, 16 * h : 16 * h + 16, :].reshape(128, 256) for h in range(2)]
    received = jnp.concatenate(
        [
            jnp.concatenate([half[:, 128 * v : 128 * v + 128] for half in halves], axis=1)
            for v in range(2)
        ],
        axis=0,
    )
    series = dot(toeplitz, received, 0, 0).astype(BF16)
    series_ref[...] = series

    part = dot(series, series, 1, 1)
    gtx[:, :, 0:128] = part[0:128, 0:128].reshape(16, 8, 128)
    gtx[:, :, 128:256] = part[128:256, 0:128].reshape(16, 8, 128)
    gtx[:, :, 256:384] = part[128:256, 128:256].reshape(16, 8, 128)
    push(yz_peers, lambda p: gtx.at[p], grx.at[yz_me], 2)
    grx[yz_me] = gtx[yz_me]
    wait(grx, len(YZ), recv_sems.at[2])
    atx[...] = jnp.sum(grx[...], axis=0)
    push(cx_peers, lambda p: atx, arx.at[cx_me], 3)
    arx[cx_me] = atx[...]
    wait(arx, len(CX), recv_sems.at[3])
    gall[yz_me] = jnp.sum(arx[...], axis=0)
    push(yz_peers, lambda p: gall.at[yz_me], gall.at[yz_me], 4)
    wait(gall, len(YZ), recv_sems.at[4])
    gram_ref[...] = gall[...].reshape(128, 384) * (1.0 / 32768.0)

    wait(tx, len(YZ), send_sems.at[0])
    wait(tx2, len(CX), send_sems.at[1])
    wait(gtx, len(YZ), send_sems.at[2])
    wait(arx, len(CX), send_sems.at[3])
    wait(gall, len(YZ), send_sems.at[4])


def spread(x):
    return jnp.broadcast_to(x, (8, 128))


def eliminate(matrices):
    tiles = 16
    lane = lax.broadcasted_iota(jnp.int32, (8, 128), 1)
    sub = lax.broadcasted_iota(jnp.int32, (8, 128), 0)
    works = [[g[8 * i : 8 * i + 8] for i in range(tiles)] for g in matrices]
    cols = [[spread(work[0][:, c : c + 1]) for c in range(8)] for work in works]
    for t in range(tiles):
        inside = (lane >= 8 * t) & (lane < 8 * t + 8)
        eye = jnp.where(lane - 8 * t == sub, 1.0, 0.0).astype(F32)
        for m, work in enumerate(works):
            col = cols[m]
            if t + 1 < tiles:
                below = work[t + 1]
                side = [spread(below[:, 8 * t + c : 8 * t + c + 1]) for c in range(8)]
                ahead = [spread(below[:, 8 * t + 8 + c : 8 * t + 9 + c]) for c in range(8)]
                below = jnp.where(inside, 0.0, below)
            base = jnp.where(inside, eye, work[t])
            row = [spread(base[r : r + 1, :]) for r in range(8)]
            inv = [None] * 8
            for s in range(8):
                inv[s] = 1.0 / spread(col[s][s : s + 1, :])
                scaled = row[s] * inv[s]
                if t + 1 < tiles:
                    below = below - side[s] * scaled
                    side_scaled = side[s] * inv[s]
                    for c in range(8):
                        ahead[c] = ahead[c] - side_scaled * spread(side[s][c : c + 1, :])
                for c in range(s + 1, 8):
                    entry = spread(col[s][c : c + 1, :])
                    col[c] = col[c] - (col[s] * entry) * inv[s]
                    row[c] = row[c] - entry * scaled
                    if t + 1 < tiles:
                        side[c] = side[c] - side[s] * (entry * inv[s])
            tile, scale = row[0], inv[0]
            for r in range(1, 8):
                tile = jnp.where(sub == r, row[r], tile)
                scale = jnp.where(sub == r, inv[r], scale)
            if t + 1 < tiles:
                work[t + 1] = below
                cols[m] = ahead
            if t + 2 < tiles:
                ah, am, al = split3(tile)
                bh, bm, bl = split3(tile * scale)
                left = jnp.concatenate([x.astype(F32) for x in (ah, ah, am, ah, al, am)], axis=0)
                right = jnp.concatenate([x.astype(F32) for x in (bh, bm, bh, bl, bh, bm)], axis=0)
                update = dot(left.astype(BF16), right.astype(BF16), 0, 0)
                for i in range(t + 2, tiles):
                    work[i] = jnp.where(inside, 0.0, work[i]) - update[8 * i : 8 * i + 8]
            work[t] = jnp.where(lane < 8 * t + 8, tile * jnp.sqrt(scale), 0.0)
    return [jnp.concatenate(work, axis=0) for work in works]


def factor_kernel(gram_ref, series_ref, sketch_ref, basis_ref, factor_ref):
    c11 = gram_ref[:, 0:128]
    c21 = gram_ref[:, 128:256]
    c22 = gram_ref[:, 256:384]
    cov = jnp.concatenate(
        [jnp.concatenate([c11, c21.T], axis=1), jnp.concatenate([c21, c22], axis=1)], axis=0
    )
    sketch = sketch_ref[...]
    w = dot_fb(cov, sketch)
    g1 = dot_fb(w, sketch, 0, 0).T
    cw = dot_ff(cov, w)
    g2 = dot_ff(w, cw, 0, 0)
    inv1, inv2 = eliminate([g1, g2])
    r = lax.broadcasted_iota(jnp.int32, (128, 128), 0)
    c = lax.broadcasted_iota(jnp.int32, (128, 128), 1)
    upper = jnp.where(c >= r, dot_ff(inv2, g2), 0.0)
    factor_ref[...] = jnp.where(c >= r, dot_ff(upper, inv1, 1, 1), 0.0)
    z = dot_ff(inv2, w, 1, 1)
    basis_ref[...] = dot_fb(z, series_ref[...])


def shards(frames, sketch, kernel_taps):
    narrow_band, broad_band = gauss_band(1.5, 256), gauss_band(3.0, 256)
    colh, coll = np_split2(np.concatenate([narrow_band, broad_band], axis=0).T)
    rowh, rowl = np_split2(np.concatenate([narrow_band, -broad_band], axis=1))
    bands = np.concatenate(
        [np.concatenate([colh, coll], axis=1), np.concatenate([rowh, rowl], axis=0)], axis=0
    )
    vmem = pl.BlockSpec(memory_space=pltpu.VMEM)
    hbm = pl.BlockSpec(memory_space=pltpu.HBM)
    gram, series = pl.pallas_call(
        exchange_kernel,
        out_shape=(
            jax.ShapeDtypeStruct((128, 384), F32),
            jax.ShapeDtypeStruct((256, 256), BF16),
        ),
        in_specs=[hbm] * 3,
        out_specs=(vmem, vmem),
        scratch_shapes=[
            pltpu.VMEM(frames.shape, BF16),
            pltpu.VMEM((1, 64), BF16),
            pltpu.VMEM(bands.shape, BF16),
            pltpu.SemaphoreType.DMA((3,)),
            pltpu.VMEM((8, 256), F32),
            pltpu.VMEM((16, 16, 256), BF16),
            pltpu.VMEM((16, 16, 256), BF16),
            pltpu.VMEM((8, 32, 256), BF16),
            pltpu.VMEM((8, 32, 256), BF16),
            pltpu.VMEM((16, 8, 384), F32),
            pltpu.VMEM((16, 8, 384), F32),
            pltpu.VMEM((8, 384), F32),
            pltpu.VMEM((8, 8, 384), F32),
            pltpu.VMEM((16, 8, 384), F32),
            pltpu.SemaphoreType.DMA((5,)),
            pltpu.SemaphoreType.DMA((5,)),
        ],
        compiler_params=pltpu.CompilerParams(
            collective_id=0, has_side_effects=True, vmem_limit_bytes=56098816
        ),
        name="exchange",
    )(frames, kernel_taps.reshape(1, 64), jnp.asarray(bands))
    return pl.pallas_call(
        factor_kernel,
        out_shape=(jax.ShapeDtypeStruct((128, 256), F32), jax.ShapeDtypeStruct((128, 128), F32)),
        in_specs=[vmem] * 3,
        out_specs=(vmem, vmem),
        compiler_params=pltpu.CompilerParams(vmem_limit_bytes=40 * 2**20),
        name="factorize",
    )(gram, series, sketch)


def solution(mesh):
    return jax.shard_map(
        shards,
        mesh=mesh,
        in_specs=(P(("wide", "narrow"), None, None, None), P(), P()),
        out_specs=(P(None, ("wide", "narrow")), P()),
        check_vma=False,
    )
```

time: 52 us -> 37.9 us (0.73)
  the two profiles are of different devices: /device:TPU:1 before, /device:TPU:0 now
where the time goes in v2:
time: 37.9 us; the launch traced here: 37.8 us
  Pallas kernels  36.5 us (96%)
  local copies, waits for them, and re-layouts  0.65 us (2%)
  between operations  0.65 us (2%)
    pallas_call x1, Pallas kernels, shards(): pl.pallas_call(exchange_kernel, out_shape=(jax.ShapeDtypeStruct((128, 384...  30.3 us
    pallas_call x1, Pallas kernels, shards(): pl.pallas_call(factor_kernel, out_shape=(jax.ShapeDtypeStruct((128, 256),...  6.16 us

profile of v2, /device:TPU:0, one launch (start us, length us, event | category | flops | bytes accessed | tf_op | source)
XLA Modules:
  0.0 37.8 jit_solution(12415639430739264655)
XLA Ops:
  0.6 0.0 copy-start.1
  0.6 0.6 %copy-done.1 = bf16[64]{0:T(256)(128)(2,1)S(1)} copy-done((bf16[64]{0:T(256)(128)(2,1)S(1)}, bf16[64]{0:T(256)(128)(2,1)}, u32[]{:S(2)}) %copy-start.1) | copy-done | bytes 152
  1.3 0.0 copy-start
  1.3 30.3 %exchange.1 = (f32[128,384]{1,0:T(8,128)S(1)}, bf16[256,256]{1,0:T(8,128)(2,1)S(1)}) custom-call(bf16[2,2,256,256]{3,2,1,0:T(8,128)(2,1)} %frames_hbm.1, bf16[1,64]{1,0:T(2,128)(2,1)S(1)} %bitcast.1, bf16[512,512]{1,0:T(8,128)(2,1)} %constant.2.clone.bands_hbm), custom_call_target="tpu_custom_call" | custom-call | tf_op jit(solution)/shard_map/exchange/pallas_call | solution.py:286
  31.6 0.0 copy-done
  31.6 6.2 %factorize.1 = (f32[128,256]{1,0:T(8,128)}, f32[128,128]{1,0:T(8,128)}) custom-call(f32[128,384]{1,0:T(8,128)S(1)} %get-tuple-element.4.gram_ref, bf16[256,256]{1,0:T(8,128)(2,1)S(1)} %get-tuple-element.5.series_ref, bf16[256,128]{1,0:T(8,128)(2,1)S(1)} %copy-done), custom_call_target="tpu_custom_call" | custom-call | tf_op jit(solution)/shard_map/factorize/pallas_call | solution.py:317
Async XLA Ops:
  0.6 0.7 %copy-start.1 = (bf16[64]{0:T(256)(128)(2,1)S(1)}, bf16[64]{0:T(256)(128)(2,1)}, u32[]{:S(2)}) copy-start(bf16[64]{0:T(256)(128)(2,1)} %param.6) | copy-start | bytes 388
  1.3 30.3 %copy-start = (bf16[256,128]{1,0:T(8,128)(2,1)S(1)}, bf16[256,128]{1,0:T(8,128)(2,1)}, u32[]{:S(2)}) copy-start(bf16[256,128]{1,0:T(8,128)(2,1)} %sketch_ref.1) | copy-start | bytes 196612

commit v3 on v2

--- a/solution.py
+++ b/solution.py
@@ -175,9 +175,13 @@
     series_ref[...] = series
 
     part = dot(series, series, 1, 1)
-    gtx[:, :, 0:128] = part[0:128, 0:128].reshape(16, 8, 128)
-    gtx[:, :, 128:256] = part[128:256, 0:128].reshape(16, 8, 128)
-    gtx[:, :, 256:384] = part[128:256, 128:256].reshape(16, 8, 128)
+    first, second = part[0:128, 0:128], part[128:256, 128:256]
+    r = lax.broadcasted_iota(jnp.int32, (128, 128), 0)
+    c = lax.broadcasted_iota(jnp.int32, (128, 128), 1)
+    diagonal = jnp.sum(jnp.where(r == c, second, 0.0), axis=0, keepdims=True)
+    gtx[:, 0:8, :] = jnp.where(r >= c, first, second).reshape(16, 8, 128)
+    gtx[:, 8:16, :] = part[128:256, 0:128].reshape(16, 8, 128)
+    gtx[:, 16:17, :] = jnp.broadcast_to(diagonal.reshape(1, 1, 128), (16, 1, 128))
     push(yz_peers, lambda p: gtx.at[p], grx.at[yz_me], 2)
     grx[yz_me] = gtx[yz_me]
     wait(grx, len(YZ), recv_sems.at[2])
@@ -185,10 +189,13 @@
     push(cx_peers, lambda p: atx, arx.at[cx_me], 3)
     arx[cx_me] = atx[...]
     wait(arx, len(CX), recv_sems.at[3])
-    gall[yz_me] = jnp.sum(arx[...], axis=0)
+    gall[yz_me] = jnp.sum(arx[...], axis=0) * (1.0 / 32768.0)
     push(yz_peers, lambda p: gall.at[yz_me], gall.at[yz_me], 4)
     wait(gall, len(YZ), recv_sems.at[4])
-    gram_ref[...] = gall[...].reshape(128, 384) * (1.0 / 32768.0)
+    gram_ref[0:128, 0:128] = gall[:, 0:8, :].reshape(128, 128)
+    gram_ref[0:128, 128:256] = gall[:, 8:16, :].reshape(128, 128)
+    gram_ref[128:136, 0:128] = jnp.broadcast_to(gall[0, 16:17, :], (8, 128))
+    gram_ref[128:136, 128:256] = jnp.zeros((8, 128), F32)
 
     wait(tx, len(YZ), send_sems.at[0])
     wait(tx2, len(CX), send_sems.at[1])
@@ -254,9 +261,12 @@
 
 
 def factor_kernel(gram_ref, series_ref, sketch_ref, basis_ref, factor_ref):
-    c11 = gram_ref[:, 0:128]
-    c21 = gram_ref[:, 128:256]
-    c22 = gram_ref[:, 256:384]
+    r = lax.broadcasted_iota(jnp.int32, (128, 128), 0)
+    c = lax.broadcasted_iota(jnp.int32, (128, 128), 1)
+    both, c21, diagonal = gram_ref[0:128, 0:128], gram_ref[0:128, 128:256], gram_ref[128:129, 0:128]
+    turned = both.T
+    c11 = jnp.where(r >= c, both, turned)
+    c22 = jnp.where(r < c, both, jnp.where(r == c, diagonal, turned))
     cov = jnp.concatenate(
         [jnp.concatenate([c11, c21.T], axis=1), jnp.concatenate([c21, c22], axis=1)], axis=0
     )
@@ -266,8 +276,6 @@
     cw = dot_ff(cov, w)
     g2 = dot_ff(w, cw, 0, 0)
     inv1, inv2 = eliminate([g1, g2])
-    r = lax.broadcasted_iota(jnp.int32, (128, 128), 0)
-    c = lax.broadcasted_iota(jnp.int32, (128, 128), 1)
     upper = jnp.where(c >= r, dot_ff(inv2, g2), 0.0)
     factor_ref[...] = jnp.where(c >= r, dot_ff(upper, inv1, 1, 1), 0.0)
     z = dot_ff(inv2, w, 1, 1)
@@ -286,7 +294,7 @@
     gram, series = pl.pallas_call(
         exchange_kernel,
         out_shape=(
-            jax.ShapeDtypeStruct((128, 384), F32),
+            jax.ShapeDtypeStruct((136, 256), F32),
             jax.ShapeDtypeStruct((256, 256), BF16),
         ),
         in_specs=[hbm] * 3,
@@ -301,11 +309,11 @@
             pltpu.VMEM((16, 16, 256), BF16),
             pltpu.VMEM((8, 32, 256), BF16),
             pltpu.VMEM((8, 32, 256), BF16),
-            pltpu.VMEM((16, 8, 384), F32),
-            pltpu.VMEM((16, 8, 384), F32),
-            pltpu.VMEM((8, 384), F32),
-            pltpu.VMEM((8, 8, 384), F32),
-            pltpu.VMEM((16, 8, 384), F32),
+            pltpu.VMEM((16, 17, 128), F32),
+            pltpu.VMEM((16, 17, 128), F32),
+            pltpu.VMEM((17, 128), F32),
+            pltpu.VMEM((8, 17, 128), F32),
+            pltpu.VMEM((16, 17, 128), F32),
             pltpu.SemaphoreType.DMA((5,)),
             pltpu.SemaphoreType.DMA((5,)),
         ],
@@ -313,7 +321,7 @@
             collective_id=0, has_side_effects=True, vmem_limit_bytes=56098816
         ),
         name="exchange",
-    )(frames, kernel_taps.reshape(1, 64), jnp.asarray(bands))
+    )(frames, pltpu.with_memory_space_constraint(kernel_taps.reshape(1, 64), pltpu.HBM), jnp.asarray(bands))
     return pl.pallas_call(
         factor_kernel,
         out_shape=(jax.ShapeDtypeStruct((128, 256), F32), jax.ShapeDtypeStruct((128, 128), F32)),

time: 37.9 us -> 36.8 us (0.971)
  Pallas kernels: 36.5 us -> 35.8 us
  local copies, waits for them, and re-layouts: 0.65 us -> 0.01 us
    unnamed x4 -> x2, local copies, waits for them, and re-layouts: 0.65 us -> 0.01 us
    pallas_call x1, Pallas kernels: 30.3 us -> 29.7 us  [shards(): pl.pallas_call(exchange_kernel, out_shape=(jax.ShapeDtypeStruct((136, 256...]
where the time goes in v3:
time: 36.8 us; the launch traced here: 36.5 us
  Pallas kernels  35.8 us (97%)
  between operations  0.65 us (2%)
    pallas_call x1, Pallas kernels, shards(): pl.pallas_call(exchange_kernel, out_shape=(jax.ShapeDtypeStruct((136, 256...  29.7 us
    pallas_call x1, Pallas kernels, shards(): pl.pallas_call(factor_kernel, out_shape=(jax.ShapeDtypeStruct((128, 256),...  6.13 us

profile of v3, /device:TPU:0, one launch (start us, length us, event | category | flops | bytes accessed | tf_op | source)
XLA Modules:
  0.0 36.5 jit_solution(18369597898100063726)
XLA Ops:
  0.6 0.0 copy-start
  0.6 29.7 %exchange.1 = (f32[136,256]{1,0:T(8,128)S(1)}, bf16[256,256]{1,0:T(8,128)(2,1)S(1)}) custom-call(bf16[2,2,256,256]{3,2,1,0:T(8,128)(2,1)} %frames_hbm.1, bf16[1,64]{1,0:T(2,128)(2,1)} %bitcast.1, bf16[512,512]{1,0:T(8,128)(2,1)} %constant.2.clone.bands_hbm), custom_call_target="tpu_custom_call" | custom-call | tf_op jit(solution)/shard_map/exchange/pallas_call | solution.py:294
  30.3 0.0 copy-done
  30.4 6.1 %factorize.1 = (f32[128,256]{1,0:T(8,128)}, f32[128,128]{1,0:T(8,128)}) custom-call(f32[136,256]{1,0:T(8,128)S(1)} %get-tuple-element.4.gram_ref, bf16[256,256]{1,0:T(8,128)(2,1)S(1)} %get-tuple-element.5.series_ref, bf16[256,128]{1,0:T(8,128)(2,1)S(1)} %copy-done), custom_call_target="tpu_custom_call" | custom-call | tf_op jit(solution)/shard_map/factorize/pallas_call | solution.py:325
Async XLA Ops:
  0.6 29.7 %copy-start = (bf16[256,128]{1,0:T(8,128)(2,1)S(1)}, bf16[256,128]{1,0:T(8,128)(2,1)}, u32[]{:S(2)}) copy-start(bf16[256,128]{1,0:T(8,128)(2,1)} %sketch_ref.1) | copy-start | bytes 196612
